TPU v7x, 32 devices: a whole 2x2x4 slice. The times are simulated.
32 devices in a mesh: seq: 8 (over y, x, core), head: 4 (over z).
Axes of the slice: x: 2, y: 2, z: 4, core: 2. Of those that a mesh axis runs over, the one named last changes fastest.
Arguments:
- queries: bfloat16 [128, 8192], P('seq', 'head'), may hold values from -130 to 130
- grad_output: bfloat16 [128, 8192], P('seq', 'head'), may hold values from -384 to 384
- key_cache: bfloat16 [3072, 512], P('seq', 'head'), may hold values from -6 to 6
- saved_value_rows: bfloat16 [3072, 512], P('seq', 'head'), may hold values from -6 to 6
- lengths: int32 [8], P('seq'), may hold values from 1 to 384, 2304 in all
- span_index: int32 [1], replicated, may hold values from 4 to 17
- w_query: bfloat16 [4096, 8192], P('seq', 'head'), may hold values from -0.09375 to 0.09375
- key_projection_weight: bfloat16 [4096, 512], P(None, 'head'), may hold values from -0.09375 to 0.09375
- value_projection_weight: bfloat16 [4096, 512], P(None, 'head'), may hold values from -0.09375 to 0.09375
Outputs:
- saved_key_gradient: bfloat16 [3072, 512], P('seq', 'head')
- saved_value_gradient: bfloat16 [3072, 512], P('seq', 'head')
- cached_input_gradient: bfloat16 [3072, 4096], P('seq', 'head')
- grad_span_input: bfloat16 [128, 4096], P('head', 'seq')
All inputs are finite; a program needn't handle non-finite values. No bound on the sum of `lengths` on one device may be relied on, other than what follows from the above.
Results may differ from a plain program's by a relative error of at most 0.02.
Values may be sent and summed in bfloat16 or wider, within the bound.
A program may use at most 64 MiB of HBM per device.

v0:
```python
import jax
import jax.numpy as jnp
from jax import lax
from jax.sharding import PartitionSpec as P

HEAD_WIDTH = 128


LOWEST_SCORE = -1e30


def prefix(part, axis, combine, identity):
    place = lax.axis_index(axis)
    gathered = lax.all_gather(part, axis)
    state = jnp.zeros_like(part) + jnp.asarray(identity, part.dtype)

    def one(lap, state):
        return combine(state, lax.dynamic_index_in_dim(gathered, lap, 0, False))

    return lax.fori_loop(0, place, one, state)


def merged(part, axis, combine):
    gathered = jax.tree.map(lambda a: lax.all_gather(a, axis), part)

    def take(source):
        return jax.tree.map(lambda a: lax.dynamic_index_in_dim(a, source, 0, False), gathered)

    return lax.fori_loop(
        1, lax.axis_size(axis), lambda source, state: combine(state, take(source)), take(0)
    )


def add_counts(earlier, later):
    return earlier + later


def pair_merge(first, second):
    joined_peak = jnp.maximum(first[0], second[0])
    first_factor = jnp.exp(first[0] - joined_peak)
    second_factor = jnp.exp(second[0] - joined_peak)
    return (joined_peak, first[1] * first_factor + second[1] * second_factor)


def local(
    queries,
    grad_output,
    key_cache,
    saved_value_rows,
    lengths,
    span_index,
    w_query,
    key_projection_weight,
    value_projection_weight,
):
    score_scale = HEAD_WIDTH ** (-0.5)
    offset = prefix(lengths, "seq", add_counts, jnp.zeros((1,), jnp.int32))
    query_all, grad_all = (
        lax.all_gather(queries, "seq", axis=0, tiled=True),
        lax.all_gather(grad_output, "seq", axis=0, tiled=True),
    )
    row_count = query_all.shape[0]
    block_size = key_cache.shape[0]
    heads_per_group = query_all.shape[1] // HEAD_WIDTH
    within = jnp.arange(block_size, dtype=jnp.int32)
    query_positions = span_index[0] * row_count + jnp.arange(row_count, dtype=jnp.int32)
    visible = (within < lengths[0])[None, :] & (
        (offset[0] + within)[None, :] <= query_positions[:, None]
    )
    visible = visible[None, :, :]
    query_heads = query_all.reshape(row_count, heads_per_group, HEAD_WIDTH)
    grad_heads = grad_all.reshape(row_count, heads_per_group, HEAD_WIDTH)
    scores = (
        jnp.einsum("ihd,pd->hip", query_heads, key_cache, preferred_element_type=jnp.float32)
        * score_scale
    )
    weight_grads = jnp.einsum(
        "ihd,pd->hip", grad_heads, saved_value_rows, preferred_element_type=jnp.float32
    )
    local_peak = jnp.max(jnp.where(visible, scores, LOWEST_SCORE), axis=2)
    local_exp = jnp.exp(jnp.where(visible, scores - local_peak[:, :, None], LOWEST_SCORE))
    local_total = jnp.sum(local_exp, axis=2)
    row_peak, row_total = merged((local_peak, local_total), "seq", pair_merge)
    weights = (
        jnp.exp(jnp.where(visible, scores - row_peak[:, :, None], LOWEST_SCORE))
        / row_total[:, :, None]
    )
    row_terms = lax.psum(jnp.sum(weights * weight_grads, axis=2), "seq")
    score_grads = weights * (weight_grads - row_terms[:, :, None])
    weights_low = weights.astype(jnp.bfloat16)
    score_low = score_grads.astype(jnp.bfloat16)
    value_grads = jnp.einsum(
        "hip,ihd->pd", weights_low, grad_heads, preferred_element_type=jnp.float32
    )
    key_grads = (
        jnp.einsum("hip,ihd->pd", score_low, query_heads, preferred_element_type=jnp.float32)
        * score_scale
    )
    query_part = (
        jnp.einsum("hip,pd->ihd", score_low, key_cache, preferred_element_type=jnp.float32)
        * score_scale
    )
    query_sum = lax.psum(query_part.reshape(row_count, heads_per_group * HEAD_WIDTH), "seq")
    query_low = query_sum.astype(jnp.bfloat16)
    span_part = jnp.dot(query_low, w_query.T, preferred_element_type=jnp.float32)
    grad_span_input = lax.psum_scatter(span_part, "head", scatter_dimension=0, tiled=True).astype(
        jnp.bfloat16
    )
    saved_key_gradient = key_grads.astype(jnp.bfloat16)
    saved_value_gradient = value_grads.astype(jnp.bfloat16)
    key_weights, value_weights = (
        lax.all_to_all(key_projection_weight, "head", split_axis=0, concat_axis=1, tiled=True),
        lax.all_to_all(value_projection_weight, "head", split_axis=0, concat_axis=1, tiled=True),
    )
    key_all, value_all = (
        lax.all_gather(saved_key_gradient, "head", axis=1, tiled=True),
        lax.all_gather(saved_value_gradient, "head", axis=1, tiled=True),
    )
    total = jnp.zeros((block_size, key_weights.shape[0]), jnp.float32)
    for member in range(lax.axis_size("head")):
        first = member * HEAD_WIDTH
        both = jnp.concatenate(
            [key_all[:, first : first + HEAD_WIDTH], value_all[:, first : first + HEAD_WIDTH]],
            axis=1,
        )
        joined = jnp.concatenate(
            [
                key_weights[:, first : first + HEAD_WIDTH],
                value_weights[:, first : first + HEAD_WIDTH],
            ],
            axis=1,
        )
        partial_term = jnp.dot(both, joined.T, preferred_element_type=jnp.float32)
        rounded = lax.optimization_barrier(partial_term.astype(jnp.bfloat16))
        total = total + rounded.astype(jnp.float32)
    cached_input_gradient = total.astype(jnp.bfloat16)
    return (saved_key_gradient, saved_value_gradient, cached_input_gradient, grad_span_input)


def solution(mesh):
    in_specs = (
        P("seq", "head"),
        P("seq", "head"),
        P("seq", "head"),
        P("seq", "head"),
        P("seq"),
        P(),
        P("seq", "head"),
        P(None, "head"),
        P(None, "head"),
    )
    out_specs = (P("seq", "head"), P("seq", "head"), P("seq", "head"), P("head", "seq"))
    return jax.shard_map(local, mesh=mesh, in_specs=in_specs, out_specs=out_specs, check_vma=False)
```

profile of v0, /device:TPU:0, one launch (start us, length us, event | category | flops | bytes accessed | tf_op | source)
XLA Modules:
  0.0 223.1 jit_solution(10164929321195194890)
XLA Ops:
  7.2 0.0 copy-start
  7.2 0.0 copy-start.5
  7.2 6.5 %all-to-all-start = ((bf16[4,1024,128]{2,1,0:T(8,128)(2,1)}), bf16[4,1024,128]{2,1,0:T(8,128)(2,1)}, u32[]{:S(2)}, u32[]{:S(2)}) async-start(bf16[4,1024,128]{2,1,0:T(8,128)(2,1)} %bitcast.106), calls=%async_computation | async-start | bytes 2097152 | tf_op jit(solution)/shard_map/all_to_all | solution.py:112
  13.7 0.0 reduce-scatter.2.cloned.1.call-start
  14.3 1.2 dynamic-slice
  15.6 0.8 dynamic-update-slice
  16.3 8.0 %all-reduce = s32[8]{0:T(128)S(1)} all-reduce(s32[8]{0:T(128)S(1)} %dynamic-update-slice), channel_id=2, replica_groups=mesh['seq'=8,'head'=4] {'seq'}, use_global_device_ids=true, to_apply=%add | all-reduce | flops 8 | bytes 64
  25.0 16.3 %all_gather.32 = bf16[128,2048]{1,0:T(8,128)(2,1)S(1)} all-gather(bf16[16,2048]{1,0:T(8,128)(2,1)} %param.13), channel_id=1, replica_groups=mesh['seq'=8,'head'=4] {'seq'}, dimensions={0}, use_global_device_ids=true | all-gather | bytes 589824 | tf_op jit(solution)/shard_map/all_gather | solution.py:59
  41.3 0.3 copy.33
  41.5 0.2 compare_and_fusion
  41.7 0.0 copy-done.5
  41.7 0.0 copy-start.12
  41.7 0.6 fusion.5
  42.3 0.0 copy-start.1
  42.3 0.0 copy-start.13
  42.3 9.1 %all-gather.1 = f32[128,128]{1,0:T(8,128)S(1)} all-gather(f32[16,128]{1,0:T(8,128)S(1)} %get-tuple-element.199), channel_id=3, replica_groups=mesh['seq'=8,'head'=4] {'seq'}, dimensions={0}, use_global_device_ids=true | all-gather | bytes 73728 | tf_op jit(solution)/shard_map/all_gather | solution.py:24
  51.4 0.0 copy-done.1
  51.4 0.7 fusion.8
  52.1 8.5 %all-gather.2 = f32[128,128]{1,0:T(8,128)S(1)} all-gather(f32[16,128]{1,0:T(8,128)S(1)} %fusion.8), channel_id=4, replica_groups=mesh['seq'=8,'head'=4] {'seq'}, dimensions={0}, use_global_device_ids=true | all-gather | bytes 73728 | tf_op jit(solution)/shard_map/all_gather | solution.py:24
  60.6 0.3 while.28
  60.9 0.0 copy-done.12
  60.9 9.6 %all_gather.37 = bf16[128,2048]{1,0:T(8,128)(2,1)S(1)} all-gather(bf16[16,2048]{1,0:T(8,128)(2,1)S(1)} %copy-done.12), channel_id=1, replica_groups=mesh['seq'=8,'head'=4] {'seq'}, dimensions={0}, use_global_device_ids=true | all-gather | bytes 589824 | tf_op jit(solution)/shard_map/all_gather | solution.py:60
  70.5 1.0 copy.35
  71.5 0.0 copy-done.13
  71.5 4.7 %fusion.2 = (f32[16,128]{1,0:T(8,128)S(1)}, f32[384,128,16]{1,0,2:T(8,128)}) fusion(f32[16,128]{1,0:T(8,128)S(1)} %get-tuple-element.162, f32[16,128]{1,0:T(8,128)S(1)} %get-tuple-element.161, f32[384,128,16]{1,0,2:T(8,128)} %copy-done.1, pred[128,384]{0,1:T(8,128)(4,1)S(1)} %compare_and_fusion, bf16[128,16,128]{0,2,1:T(8,128)(2,1)} %bitcast.108, ...), kind=kOutput, calls=%fused_computation.8 | convolution fusion | flops 206043136 | bytes 6987776 | tf_op jit(solution)/shard_map/ihd,pd->hip/dot_general | solution.py:77
  76.1 13.4 %psum.14 = f32[16,128]{1,0:T(8,128)S(1)} all-reduce(f32[16,128]{1,0:T(8,128)S(1)} %get-tuple-element.201), channel_id=1, replica_groups=mesh['seq'=8,'head'=4] {'seq'}, use_global_device_ids=true, to_apply=%region_7.8 | all-reduce | flops 2048 | bytes 16384 | tf_op jit(solution)/shard_map/psum | solution.py:88
  89.6 3.9 %fusion.4 = bf16[16,128,384]{1,2,0:T(8,128)(2,1)S(1)} fusion(f32[384,128,16]{1,0,2:T(8,128)} %get-tuple-element.202, f32[16,128]{1,0:T(8,128)S(1)} %psum.14, f32[16,128]{1,0:T(8,128)S(1)} %get-tuple-element.162, f32[16,128]{1,0:T(8,128)S(1)} %get-tuple-element.161, f32[384,128,16]{1,0,2:T(8,128)} %copy-done.1, pred[128,384]{0,1:T(8,128)(4,1)S(1)} %compare_and_fusion), kind=kLoop, calls=%fused_computation.10 | loop fusion | flops 5505024 | bytes 7938048 | tf_op jit(solution)/shard_map/convert_element_type | solution.py:91
  93.4 0.0 copy-start.2
  93.5 1.2 copy-done.2
  94.6 1.5 convolution_multiply_fusion
  96.1 51.0 %all-reduce.2 = bf16[128,2048]{0,1:T(8,128)(2,1)S(1)} all-reduce(f32[128,2048]{0,1:T(8,128)} %bitcast.105), channel_id=1, replica_groups=mesh['seq'=8,'head'=4] {'seq'}, use_global_device_ids=true, to_apply=%region_8.9 | all-reduce | flops 262144 | bytes 1572864 | tf_op jit(solution)/shard_map/psum | solution.py:103
  147.1 0.0 copy-done
  147.1 1.5 fusion.62
  148.6 0.0 reduce-scatter.2.cloned.1.call-update
  148.7 0.0 all-to-all-done
  148.7 5.1 %all-to-all-start.1 = ((bf16[4,1024,128]{2,1,0:T(8,128)(2,1)}), bf16[4,1024,128]{2,1,0:T(8,128)(2,1)}, u32[]{:S(2)}, u32[]{:S(2)}) async-start(bf16[4,1024,128]{2,1,0:T(8,128)(2,1)} %bitcast.107), calls=%async_computation.1 | async-start | bytes 2097152 | tf_op jit(solution)/shard_map/all_to_all | solution.py:113
  153.8 3.0 %fusion.18 = bf16[384,128]{1,0:T(8,128)(2,1)S(1)} fusion(bf16[128,16,128]{0,2,1:T(8,128)(2,1)} %bitcast.109, f32[384,128,16]{1,0,2:T(8,128)} %copy-done.1, f32[16,128]{1,0:T(8,128)S(1)} %get-tuple-element.162, f32[16,128]{1,0:T(8,128)S(1)} %get-tuple-element.161, pred[128,384]{0,1:T(8,128)(4,1)S(1)} %compare_and_fusion), kind=kOutput, calls=%fused_computation.32 | convolution fusion | flops 205307904 | bytes 3833856 | tf_op jit(solution)/shard_map/hip,ihd->pd/dot_general | solution.py:92
  156.8 0.0 copy-start.11
  156.8 32.6 %all_gather.39 = bf16[384,512]{1,0:T(8,128)(2,1)S(1)} all-gather(bf16[384,128]{1,0:T(8,128)(2,1)S(1)} %fusion.18), channel_id=1, replica_groups=mesh['seq'=8,'head'=4] {'head'}, dimensions={1}, use_global_device_ids=true | all-gather | bytes 491520 | tf_op jit(solution)/shard_map/all_gather | solution.py:117
  189.4 0.0 copy-done.3
  189.4 0.6 fusion.21
  190.0 0.0 copy-start.4
  190.0 14.9 %all_gather.38 = bf16[384,512]{1,0:T(8,128)(2,1)S(1)} all-gather(bf16[384,128]{1,0:T(8,128)(2,1)S(1)} %fusion.21), channel_id=1, replica_groups=mesh['seq'=8,'head'=4] {'head'}, dimensions={1}, use_global_device_ids=true | all-gather | bytes 491520 | tf_op jit(solution)/shard_map/all_gather | solution.py:116
  204.9 0.7 fusion.61
  205.6 0.7 fusion.60
  206.4 1.5 convert_element_type.59
  207.8 0.0 copy-done.11
  207.8 1.5 copy.39
  209.3 0.0 all-to-all-done.1
  209.3 2.3 %copy.40 = bf16[1024,4,128]{0,2,1:T(8,128)(2,1)} copy(bf16[1024,4,128]{2,0,1:T(8,128)(2,1)} %bitcast.22) | data formatting | bytes 2097152 | tf_op jit(solution)/shard_map/all_to_all | solution.py:113
  211.6 0.0 copy-done.4
  211.6 0.0 copy-start.6
  211.6 0.0 copy-start.9
  211.6 0.0 copy-start.7
  211.6 1.5 fusion.58
  213.1 0.0 copy-done.8
  213.1 0.0 copy-done.10
  213.1 0.4 convolution_convert_fusion.3
  213.5 0.0 copy-done.6
  213.5 0.0 copy-done.9
  213.5 0.4 convolution_convert_fusion.2
  213.9 0.4 convolution_convert_fusion.1
  214.3 0.4 convolution_convert_fusion
  214.7 1.5 add_convert_fusion
  (19 shorter events, 0.2 us)
Async XLA Ops:
  7.2 139.9 %copy-start = (bf16[512,2048]{1,0:T(8,128)(2,1)S(1)}, bf16[512,2048]{1,0:T(8,128)(2,1)}, u32[]{:S(2)}) copy-start(bf16[512,2048]{1,0:T(8,128)(2,1)} %param.19) | copy-start | bytes 6291460
  7.2 34.5 %copy-start.5 = (bf16[384,128]{1,0:T(8,128)(2,1)S(1)}, bf16[384,128]{1,0:T(8,128)(2,1)}, u32[]{:S(2)}) copy-start(bf16[384,128]{1,0:T(8,128)(2,1)} %param.15) | copy-start | bytes 294916
  7.2 141.5 %all-to-all-start = ((bf16[4,1024,128]{2,1,0:T(8,128)(2,1)}), bf16[4,1024,128]{2,1,0:T(8,128)(2,1)}, u32[]{:S(2)}, u32[]{:S(2)}) async-start(bf16[4,1024,128]{2,1,0:T(8,128)(2,1)} %bitcast.106), calls=%async_computation | async-start | bytes 2097152 | tf_op jit(solution)/shard_map/all_to_all | solution.py:112
  13.7 192.7 %reduce-scatter.2.cloned.1.call-start = ((), (), s32[]{:S(2)}) async-start(), calls=%async_computation.3 | async-start | bytes 327680 | tf_op jit(solution)/shard_map/reduce_scatter | solution.py:106
  41.7 19.2 %copy-start.12 = (bf16[16,2048]{1,0:T(8,128)(2,1)S(1)}, bf16[16,2048]{1,0:T(8,128)(2,1)}, u32[]{:S(2)}) copy-start(bf16[16,2048]{1,0:T(8,128)(2,1)} %param.14) | copy-start | bytes 196612
  42.3 9.1 %copy-start.1 = (f32[384,128,16]{1,0,2:T(8,128)}, f32[384,128,16]{1,0,2:T(8,128)S(1)}, u32[]{:S(2)}) copy-start(f32[384,128,16]{1,0,2:T(8,128)S(1)} %get-tuple-element.200) | copy-start | bytes 9437188
  42.3 29.1 %copy-start.13 = (bf16[384,128]{1,0:T(8,128)(2,1)S(1)}, bf16[384,128]{1,0:T(8,128)(2,1)}, u32[]{:S(2)}) copy-start(bf16[384,128]{1,0:T(8,128)(2,1)} %param.16) | copy-start | bytes 294916
  93.4 1.2 copy-start.2
  148.7 60.6 %all-to-all-start.1 = ((bf16[4,1024,128]{2,1,0:T(8,128)(2,1)}), bf16[4,1024,128]{2,1,0:T(8,128)(2,1)}, u32[]{:S(2)}, u32[]{:S(2)}) async-start(bf16[4,1024,128]{2,1,0:T(8,128)(2,1)} %bitcast.107), calls=%async_computation.1 | async-start | bytes 2097152 | tf_op jit(solution)/shard_map/all_to_all | solution.py:113
  153.8 35.6 %copy-start.3 = (bf16[16,128,384]{1,2,0:T(8,128)(2,1)S(1)}, bf16[16,128,384]{1,2,0:T(8,128)(2,1)}, u32[]{:S(2)}) copy-start(bf16[16,128,384]{1,2,0:T(8,128)(2,1)} %copy-done.2) | copy-start | bytes 4718596
  156.8 51.0 %copy-start.11 = (bf16[384,128]{1,0:T(8,128)(2,1)}, bf16[384,128]{1,0:T(8,128)(2,1)S(1)}, u32[]{:S(2)}) copy-start(bf16[384,128]{1,0:T(8,128)(2,1)S(1)} %fusion.18) | copy-start | bytes 294916
  190.0 21.6 %copy-start.4 = (bf16[384,128]{1,0:T(8,128)(2,1)}, bf16[384,128]{1,0:T(8,128)(2,1)S(1)}, u32[]{:S(2)}) copy-start(bf16[384,128]{1,0:T(8,128)(2,1)S(1)} %fusion.21) | copy-start | bytes 294916
  211.6 1.5 copy-start.8
  211.6 1.5 copy-start.10
  211.6 1.9 copy-start.6
  211.6 1.9 copy-start.9
  211.6 2.3 %copy-start.7 = (bf16[384,128]{1,0:T(8,128)(2,1)S(1)}, bf16[384,128]{1,0:T(8,128)(2,1)}, u32[]{:S(2)}) copy-start(bf16[384,128]{1,0:T(8,128)(2,1)} %get-tuple-element.193) | copy-start | bytes 294916
Sparse Core Ops, SparseCore 0:
  148.8 22.1 reduce-scatter.1
where the time goes:
time: 224 us; the launch traced here: 223 us
  blocking collectives  163 us (73%)
  between operations  15.6 us (7%)
  matrix products  13.4 us (6%)
  starting transfers between devices  11.6 us (5%)
  local copies, waits for them, and re-layouts  11.2 us (5%)
  other arithmetic  7.8 us (3%)
    psum x1, blocking collectives, local(): lax.psum(query_part.reshape(row_count, heads_per_group * HEAD_WIDTH), 'seq')  51 us
    all_gather x1, blocking collectives, local(): lax.all_gather(saved_value_gradient, 'head', axis=1, tiled=True)  32.6 us
    all_gather x2, blocking collectives, merged(): gathered = jax.tree.map(lambda a: lax.all_gather(a, axis), part)  17.6 us
    all_gather x1, blocking collectives, local(): lax.all_gather(queries, 'seq', axis=0, tiled=True)  16.3 us
    all_gather x1, blocking collectives, local(): lax.all_gather(saved_key_gradient, 'head', axis=1, tiled=True)  14.9 us
    psum x1, blocking collectives, local(): row_terms = lax.psum(jnp.sum(weights * weight_grads, axis=2), 'seq')  13.4 us
    all_gather x1, blocking collectives, local(): lax.all_gather(grad_output, 'seq', axis=0, tiled=True)  9.55 us
    unnamed x1, blocking collectives  8.01 us
  transfers between devices with their start and end apart: 3, of which 0 were waited for; matrix products, arithmetic and copies ran while one was open for 11% of the time, Pallas kernels for 0%

commit v1 on v0

--- a/solution.py
+++ b/solution.py
@@ -1,12 +1,434 @@
+import functools
+import math
+
 import jax
 import jax.numpy as jnp
 from jax import lax
+from jax.experimental import pallas as pl
+from jax.experimental.pallas import tpu as pltpu
 from jax.sharding import PartitionSpec as P
 
 HEAD_WIDTH = 128
 
 
 LOWEST_SCORE = -1e30
+PEAK_FLOOR = -1e29
+MESH = pl.DeviceIdType.MESH
+NT = (((1,), (1,)), ((), ()))
+
+
+def dot_nt(a, b):
+    return lax.dot_general(a, b, NT, preferred_element_type=jnp.float32)
+
+
+def dot_nn(a, b):
+    return jnp.dot(a, b, preferred_element_type=jnp.float32)
+
+
+def kernel(
+    n, nh,
+    q_in, g_in, k_ref, v_ref, len_ref, span_ref, wq_in, kw_in, vw_in,
+    dk_out, dv_out, cached_out, span_out,
+    q_all, g_all, kt, len_all, bias, e_buf, dp_buf, st_all, fac, rterm,
+    dv_acc, dk_acc, dq_send, dq_recv, dq_all, wq, w_all, dkv_all, acc,
+    span_acc, span_send, span_recv,
+    loc_sem, q_sem, g_sem, a_sem, len_sem, st_sem, rs_sem, w_sem, wf_sem, z_sem, h_sem,
+):
+    me, hd = lax.axis_index("seq"), lax.axis_index("head")
+    nchip = n // 2
+    core, chip = lax.rem(me, 2), me // 2
+    sib = me + 1 - 2 * core
+    rows_own = q_in.shape[0]
+    rows = rows_own * n
+    slots = k_ref.shape[0]
+    heads = q_in.shape[1] // HEAD_WIDTH
+    hb = heads // n
+    wid = hb * HEAD_WIDTH
+    half_rows = heads // 2
+    feats = kw_in.shape[0] // nh
+    fh = feats // 2
+    scale = HEAD_WIDTH ** (-0.5)
+
+    def seq_peer(k):
+        return lax.rem(me + k, n)
+
+    def seq_from(k):
+        return lax.rem(me + n - k, n)
+
+    def head_peer(k):
+        return lax.rem(hd + k, nh)
+
+    def head_from(k):
+        return lax.rem(hd + nh - k, nh)
+
+    def remote(src, dst, ssem, rsem, s, h):
+        return pltpu.make_async_remote_copy(
+            src_ref=src, dst_ref=dst, send_sem=ssem, recv_sem=rsem,
+            device_id=(s, h), device_id_type=MESH,
+        )
+
+    own_rows = pl.ds(pl.multiple_of(me * rows_own, rows_own), rows_own)
+    own_feats = pl.ds(pl.multiple_of(hd * feats, feats), feats)
+    local = [
+        pltpu.make_async_copy(q_in, q_all.at[own_rows], loc_sem.at[0]),
+        pltpu.make_async_copy(g_in, g_all.at[own_rows], loc_sem.at[1]),
+        pltpu.make_async_copy(wq_in, wq, loc_sem.at[2]),
+        pltpu.make_async_copy(kw_in.at[own_feats], w_all.at[2 * hd], loc_sem.at[3]),
+        pltpu.make_async_copy(vw_in.at[own_feats], w_all.at[2 * hd + 1], loc_sem.at[4]),
+    ]
+    for c in local:
+        c.start()
+    len_all[me] = jnp.full((8, 128), len_ref[0], jnp.int32)
+
+    barrier = pltpu.get_barrier_semaphore()
+    for k in range(1, n):
+        pl.semaphore_signal(barrier, inc=1, device_id=(seq_peer(k), hd), device_id_type=MESH)
+    for k in range(1, nh):
+        pl.semaphore_signal(barrier, inc=1, device_id=(me, head_peer(k)), device_id_type=MESH)
+    pl.semaphore_wait(barrier, n - 1 + nh - 1)
+
+    def chip_peer(k):
+        return 2 * lax.rem(chip + k, nchip) + core
+
+    def chip_from(k):
+        return 2 * lax.rem(chip + nchip - k, nchip) + core
+
+    def gather_copy(k, src, slot, sem):
+        to = sib if k == 0 else chip_peer(k)
+        return remote(src, slot(me), sem.at[0, k], sem.at[1, k], to, hd)
+
+    def forward_copy(k, slot, sem):
+        block = slot(chip_from(k))
+        return remote(block, block, sem.at[2, k], sem.at[3, k], sib, hd)
+
+    def gather_start(src, slot, sem):
+        for k in range(nchip):
+            gather_copy(k, src, slot, sem).start()
+
+    def gather_relay(src, slot, sem):
+        for k in range(1, nchip):
+            gather_copy(k, src, slot, sem).wait_recv()
+            forward_copy(k, slot, sem).start()
+
+    def gather_finish(src, slot, sem):
+        gather_copy(0, src, slot, sem).wait_recv()
+        for k in range(1, nchip):
+            forward_copy(k, slot, sem).wait_recv()
+
+    def gather_drain(src, slot, sem):
+        for k in range(nchip):
+            gather_copy(k, src, slot, sem).wait_send()
+        for k in range(1, nchip):
+            forward_copy(k, slot, sem).wait_send()
+
+    def row_slot(buf):
+        return lambda s: buf.at[pl.ds(pl.multiple_of(s * rows_own, rows_own), rows_own)]
+
+    q_args = (q_in, row_slot(q_all), q_sem)
+    g_args = (g_in, row_slot(g_all), g_sem)
+    a_args = (dq_all.at[me], lambda s: dq_all.at[s], a_sem)
+
+    def len_copy(k):
+        return remote(
+            len_all.at[me], len_all.at[me], len_sem.at[0, k], len_sem.at[1, k], seq_peer(k), hd
+        )
+
+    gather_start(*q_args)
+    for k in range(1, n):
+        len_copy(k).start()
+    gather_start(*g_args)
+
+    core_feats = pl.ds(pl.multiple_of(core * fh, fh), fh)
+
+    def weight_copy(k, which):
+        to = head_peer(k)
+        src = (kw_in, vw_in)[which].at[pl.ds(pl.multiple_of(to * feats + core * fh, fh), fh)]
+        return remote(
+            src, w_all.at[2 * hd + which, core_feats],
+            w_sem.at[0, which, k], w_sem.at[1, which, k], me, to,
+        )
+
+    def weight_forward(k):
+        block = w_all.at[pl.ds(2 * head_from(k), 2), core_feats]
+        return remote(block, block, wf_sem.at[0, k], wf_sem.at[1, k], sib, hd)
+
+    for k in range(1, nh):
+        for which in range(2):
+            weight_copy(k, which).start()
+
+    kt[...] = k_ref[...].T
+    gather_relay(*q_args)
+    gather_relay(*g_args)
+
+    for k in range(1, n):
+        len_copy(k).wait_recv()
+    offset = jnp.zeros((8, 128), jnp.int32)
+    for t in range(n):
+        offset = offset + len_all[t] * (t < me).astype(jnp.int32)
+    within = lax.broadcasted_iota(jnp.int32, (slots, rows), 0)
+    qpos = span_ref[0] * rows + lax.broadcasted_iota(jnp.int32, (slots, rows), 1)
+    visible = (within < len_ref[0]) & (offset[0:1, 0:1] + within <= qpos)
+    bias[...] = jnp.where(visible, 0.0, LOWEST_SCORE)
+
+    local[0].wait()
+    local[1].wait()
+    gather_finish(*q_args)
+    gather_finish(*g_args)
+
+    def pair(buf, j):
+        block = buf[:, pl.ds(pl.multiple_of(j * wid, wid), wid)]
+        return jnp.concatenate(
+            [block[:, i * HEAD_WIDTH : (i + 1) * HEAD_WIDTH] for i in range(hb)], axis=0
+        )
+
+    def st_copy(half, k):
+        return remote(
+            st_all.at[half, me], st_all.at[half, me],
+            st_sem.at[0, half, k], st_sem.at[1, half, k], seq_peer(k), hd,
+        )
+
+    for half in range(2):
+
+        def first(i, carry, half=half):
+            place = lax.rem(chip + 1 + i, nchip)
+            j = 2 * place + half
+            s = dot_nt(k_ref[...], pair(q_all, j)) * (scale * math.log2(math.e))
+            s = s + jnp.concatenate([bias[...]] * hb, axis=1)
+            m = jnp.maximum(jnp.max(s, axis=0, keepdims=True), PEAK_FLOOR)
+            e = jnp.exp2(s - m)
+            dp = dot_nt(v_ref[...], pair(g_all, j))
+            e_buf[j] = e
+            dp_buf[j] = dp
+            stats = (m, jnp.sum(e, axis=0, keepdims=True), jnp.sum(e * dp, axis=0, keepdims=True))
+            for at, stat in enumerate(stats):
+                for h in range(hb):
+                    st_all[half, me, pl.ds(at * half_rows + place * hb + h, 1), :] = stat[
+                        :, h * rows : (h + 1) * rows
+                    ]
+            return carry
+
+        lax.fori_loop(0, nchip, first, 0)
+        for k in range(1, n):
+            st_copy(half, k).start()
+
+    def rs_copy(k, to):
+        return remote(dq_send.at[to], dq_recv.at[me], rs_sem.at[0, k], rs_sem.at[1, k], to, hd)
+
+    dv_acc[...] = jnp.zeros_like(dv_acc)
+    dk_acc[...] = jnp.zeros_like(dk_acc)
+    for half in range(2):
+        for k in range(1, n):
+            st_copy(half, k).wait_recv()
+        part = lambda t, at: st_all[half, t, at * half_rows : (at + 1) * half_rows, :]
+        peak = part(0, 0)
+        for t in range(1, n):
+            peak = jnp.maximum(peak, part(t, 0))
+        total = jnp.zeros_like(peak)
+        numer = jnp.zeros_like(peak)
+        for t in range(n):
+            f = jnp.exp2(part(t, 0) - peak)
+            total = total + part(t, 1) * f
+            numer = numer + part(t, 2) * f
+        fac[half] = jnp.exp2(part(me, 0) - peak) / total
+        rterm[half] = numer / total
+
+        def second(i, carry, half=half):
+            place = lax.rem(chip + 1 + i, nchip)
+            j = 2 * place + half
+            line = lambda ref: jnp.concatenate(
+                [ref[half, pl.ds(place * hb + h, 1), :] for h in range(hb)], axis=1
+            )
+            p = e_buf[j] * line(fac)
+            ds = (p * (dp_buf[j] - line(rterm))).astype(jnp.bfloat16)
+            dv_acc[...] += dot_nn(p.astype(jnp.bfloat16), pair(g_all, j))
+            dq_send[j] = (dot_nn(kt[...], ds) * scale).astype(jnp.bfloat16)
+
+            @pl.when(j != me)
+            def _():
+                rs_copy(lax.rem(j + n - me, n), j).start()
+
+            dk_acc[...] += dot_nn(ds, pair(q_all, j))
+            return carry
+
+        lax.fori_loop(0, nchip, second, 0)
+
+    dk_low = (dk_acc[...] * scale).astype(jnp.bfloat16)
+    dv_low = dv_acc[...].astype(jnp.bfloat16)
+    dkv_all[2 * hd] = dk_low
+    dkv_all[2 * hd + 1] = dv_low
+
+    def z_copy(k):
+        block = dkv_all.at[pl.ds(2 * hd, 2)]
+        return remote(block, block, z_sem.at[0, k], z_sem.at[1, k], me, head_peer(k))
+
+    for k in range(1, nh):
+        z_copy(k).start()
+    dk_out[...] = dk_low
+    dv_out[...] = dv_low
+
+    total = dq_send[me].astype(jnp.float32)
+    for k in range(1, n):
+        rs_copy(k, seq_peer(k)).wait_recv()
+        total = total + dq_recv[seq_from(k)].astype(jnp.float32)
+    for h in range(hb):
+        dq_all[me, :, h * HEAD_WIDTH : (h + 1) * HEAD_WIDTH] = (
+            total[:, h * rows : (h + 1) * rows].T.astype(jnp.bfloat16)
+        )
+    gather_start(*a_args)
+
+    for k in range(1, nh):
+        weight_copy(k, 0).wait_recv()
+        weight_copy(k, 1).wait_recv()
+        weight_forward(k).start()
+
+    local[3].wait()
+    local[4].wait()
+    tile = min(256, feats)
+
+    def term(g, start, last):
+        lhs = jnp.concatenate([dkv_all[2 * g], dkv_all[2 * g + 1]], axis=1)
+
+        def one(i, carry):
+            at = pl.ds(pl.multiple_of(i * tile, tile), tile)
+            rhs = jnp.concatenate([w_all[2 * g, at, :], w_all[2 * g + 1, at, :]], axis=1)
+            x = dot_nt(lhs, rhs)
+            if not start:
+                x = x + acc[:, at]
+            if last:
+                cached_out[:, at] = x.astype(cached_out.dtype)
+            else:
+                acc[:, at] = x
+            return carry
+
+        lax.fori_loop(0, feats // tile, one, 0)
+
+    local[2].wait()
+    gather_relay(*a_args)
+    term(hd, True, nh == 1)
+
+    def span_add(s):
+        cols = pl.ds(pl.multiple_of(s * wid, wid), wid)
+        return dot_nt(dq_all[s], wq[:, cols])
+
+    span_acc[...] = span_add(me)
+    for k in range(1, nchip):
+        span_acc[...] += span_add(chip_from(k))
+    gather_finish(*a_args)
+
+    def other(i, carry):
+        span_acc[...] += span_add(2 * i + 1 - core)
+        return carry
+
+    lax.fori_loop(0, nchip, other, 0)
+
+    span_rows = rows // nh
+    span_send[...] = span_acc[...].astype(jnp.bfloat16).reshape(span_send.shape)
+
+    def h_copy(k):
+        to = head_peer(k)
+        return remote(span_send.at[to], span_recv.at[hd], h_sem.at[0, k], h_sem.at[1, k], me, to)
+
+    for k in range(1, nh):
+        h_copy(k).start()
+
+    for k in range(1, nh):
+        weight_forward(k).wait_recv()
+        z_copy(k).wait_recv()
+        term(head_from(k), False, k == nh - 1)
+
+    own_span = pl.ds(pl.multiple_of(hd * span_rows, span_rows), span_rows)
+    total = span_acc[own_span, :]
+    for k in range(1, nh):
+        h_copy(k).wait_recv()
+        total = total + span_recv[head_from(k)].astype(jnp.float32)
+    span_out[...] = total.astype(span_out.dtype)
+
+    gather_drain(*q_args)
+    gather_drain(*g_args)
+    gather_drain(*a_args)
+    for k in range(1, n):
+        len_copy(k).wait_send()
+        rs_copy(k, seq_peer(k)).wait_send()
+        for half in range(2):
+            st_copy(half, k).wait_send()
+    for k in range(1, nh):
+        weight_copy(k, 0).wait_send()
+        weight_copy(k, 1).wait_send()
+        weight_forward(k).wait_send()
+        z_copy(k).wait_send()
+        h_copy(k).wait_send()
+
+
+def fused(
+    n, nh, queries, grad_output, key_cache, saved_value_rows, lengths, span_index,
+    w_query, key_projection_weight, value_projection_weight,
+):
+    rows_own, width = queries.shape
+    rows, heads = rows_own * n, width // HEAD_WIDTH
+    wid = width // n
+    slots = key_cache.shape[0]
+    feats = key_projection_weight.shape[0] // nh
+    out_feats = w_query.shape[0]
+    nchip = n // 2
+    bf, f32 = jnp.bfloat16, jnp.float32
+    vmem = pl.BlockSpec(memory_space=pltpu.VMEM)
+    smem = pl.BlockSpec(memory_space=pltpu.SMEM)
+    anym = pl.BlockSpec(memory_space=pl.ANY)
+    dma = pltpu.SemaphoreType.DMA
+    V = pltpu.VMEM
+    hq = wid // HEAD_WIDTH * rows
+    return pl.pallas_call(
+        functools.partial(kernel, n, nh),
+        out_shape=(
+            jax.ShapeDtypeStruct((slots, HEAD_WIDTH), bf),
+            jax.ShapeDtypeStruct((slots, HEAD_WIDTH), bf),
+            jax.ShapeDtypeStruct((slots, feats), bf),
+            jax.ShapeDtypeStruct((rows // nh, out_feats), bf),
+        ),
+        in_specs=[anym, anym, vmem, vmem, smem, smem, anym, anym, anym],
+        out_specs=(vmem, vmem, vmem, vmem),
+        scratch_shapes=[
+            V((rows, width), bf),
+            V((rows, width), bf),
+            V((HEAD_WIDTH, slots), bf),
+            V((n, 8, 128), jnp.int32),
+            V((slots, rows), f32),
+            V((n, slots, hq), f32),
+            V((n, slots, hq), f32),
+            V((2, n, 3 * heads // 2, rows), f32),
+            V((2, heads // 2, rows), f32),
+            V((2, heads // 2, rows), f32),
+            V((slots, HEAD_WIDTH), f32),
+            V((slots, HEAD_WIDTH), f32),
+            V((n, HEAD_WIDTH, hq), bf),
+            V((n, HEAD_WIDTH, hq), bf),
+            V((n, rows, wid), bf),
+            V((out_feats, width), bf),
+            V((2 * nh, feats, HEAD_WIDTH), bf),
+            V((2 * nh, slots, HEAD_WIDTH), bf),
+            V((slots, feats), f32),
+            V((rows, out_feats), f32),
+            V((nh, rows // nh, out_feats), bf),
+            V((nh, rows // nh, out_feats), bf),
+            dma((5,)),
+            dma((4, nchip)),
+            dma((4, nchip)),
+            dma((4, nchip)),
+            dma((2, n)),
+            dma((2, 2, n)),
+            dma((2, n)),
+            dma((2, 2, nh)),
+            dma((2, nh)),
+            dma((2, nh)),
+            dma((2, nh)),
+        ],
+        compiler_params=pltpu.CompilerParams(
+            collective_id=0, has_side_effects=True, vmem_limit_bytes=48 * 1024 * 1024
+        ),
+    )(
+        queries, grad_output, key_cache, saved_value_rows, lengths, span_index,
+        w_query, key_projection_weight, value_projection_weight,
+    )
 
 
 def prefix(part, axis, combine, identity):
@@ -150,4 +572,21 @@
         P(None, "head"),
     )
     out_specs = (P("seq", "head"), P("seq", "head"), P("seq", "head"), P("head", "seq"))
-    return jax.shard_map(local, mesh=mesh, in_specs=in_specs, out_specs=out_specs, check_vma=False)
+    n, nh = mesh.shape["seq"], mesh.shape["head"]
+
+    def device(queries, *rest):
+        rows_own, width = queries.shape
+        rows, heads = rows_own * n, width // HEAD_WIDTH
+        fits = (
+            n % 2 == 0
+            and rows_own % 16 == 0
+            and rows % 128 == 0
+            and heads % n == 0
+            and (heads // 2) % 8 == 0
+            and (rows // nh) % 16 == 0
+        )
+        if not fits:
+            return local(queries, *rest)
+        return fused(n, nh, queries, *rest)
+
+    return jax.shard_map(device, mesh=mesh, in_specs=in_specs, out_specs=out_specs, check_vma=False)

time: 224 us -> 63.8 us (0.28)
  blocking collectives: 163 us -> 0 us
  Pallas kernels: 0 us -> 51.2 us
  between operations: 15.6 us -> 1.95 us
  matrix products: 13.4 us -> 0 us
  starting transfers between devices: 11.6 us -> 0 us
  other arithmetic: 7.8 us -> 0 us
    all_gather x6 -> x0, blocking collectives: 90.9 us -> none  [the longest x1 32.6 us: local(): lax.all_gather(saved_value_gradient, 'head', axis=1, tiled=True)]
    psum x2 -> x0, blocking collectives: 64.4 us -> none  [the longest x1 51 us: local(): lax.psum(query_part.reshape(row_count, heads_per_group * HEAD_WIDTH), 'seq')]
    pallas_call x0 -> x1, Pallas kernels: none -> 51.2 us  [fused(): pl.pallas_call(functools.partial(kernel, n, nh), out_shape=(jax.ShapeDtyp...]
    dot_general x10 -> x0, matrix products: 13.4 us -> none  [the longest x1 4.67 us: local(): jnp.einsum('ihd,pd->hip', grad_heads, saved_value_rows, preferred_element...]
    all_to_all x2 -> x0, starting transfers between devices: 11.6 us -> none  [the longest x1 6.46 us: local(): lax.all_to_all(key_projection_weight, 'head', split_axis=0, concat_axis=1...]
    unnamed x1 -> x0, blocking collectives: 8.01 us -> none
    unnamed x31 -> x18, local copies, waits for them, and re-layouts: 3.22 us -> 10.3 us
    convert_element_type x3 -> x0, other arithmetic: 6.83 us -> none  [the longest x1 3.86 us: local(): score_low = score_grads.astype(jnp.bfloat16)]
  transfers between devices with their start and end apart: 3 -> 0, of which waited for: 0 -> 0; matrix products, arithmetic and copies ran while one was open for 11% -> 0% of each run, Pallas kernels for 0% -> 0%
where the time goes in v1:
time: 63.8 us; the launch traced here: 63.4 us
  Pallas kernels  51.2 us (80%)
  local copies, waits for them, and re-layouts  10.3 us (16%)
  between operations  1.95 us (3%)
    pallas_call x1, Pallas kernels, fused(): pl.pallas_call(functools.partial(kernel, n, nh), out_shape=(jax.ShapeDtyp...  51.2 us
    unnamed x18, local copies, waits for them, and re-layouts  10.3 us

profile of v1, /device:TPU:0, one launch (start us, length us, event | category | flops | bytes accessed | tf_op | source)
XLA Modules:
  0.0 63.4 jit_solution(2428975350488050752)
XLA Ops:
  1.9 0.0 copy-start
  1.9 1.6 %copy-done = bf16[512,2048]{1,0:T(8,128)(2,1)S(1)} copy-done((bf16[512,2048]{1,0:T(8,128)(2,1)S(1)}, bf16[512,2048]{1,0:T(8,128)(2,1)}, u32[]{:S(2)}) %copy-start) | copy-done | bytes 2097176
  3.5 0.0 copy-start.1
  3.5 1.2 %copy-done.1 = bf16[4096,128]{1,0:T(8,128)(2,1)S(1)} copy-done((bf16[4096,128]{1,0:T(8,128)(2,1)S(1)}, bf16[4096,128]{1,0:T(8,128)(2,1)}, u32[]{:S(2)}) %copy-start.1) | copy-done | bytes 1048600
  4.7 0.0 copy-start.2
  4.7 1.2 %copy-done.2 = bf16[4096,128]{1,0:T(8,128)(2,1)S(1)} copy-done((bf16[4096,128]{1,0:T(8,128)(2,1)S(1)}, bf16[4096,128]{1,0:T(8,128)(2,1)}, u32[]{:S(2)}) %copy-start.2) | copy-done | bytes 1048600
  6.0 0.0 copy-start.3
  6.0 0.9 %copy-done.3 = bf16[384,128]{1,0:T(8,128)(2,1)S(1)} copy-done((bf16[384,128]{1,0:T(8,128)(2,1)S(1)}, bf16[384,128]{1,0:T(8,128)(2,1)}, u32[]{:S(2)}) %copy-start.3) | copy-done | bytes 98328
  6.9 0.0 copy-start.4
  6.9 0.9 %copy-done.4 = bf16[384,128]{1,0:T(8,128)(2,1)S(1)} copy-done((bf16[384,128]{1,0:T(8,128)(2,1)S(1)}, bf16[384,128]{1,0:T(8,128)(2,1)}, u32[]{:S(2)}) %copy-start.4) | copy-done | bytes 98328
  7.8 0.0 copy-start.5
  7.8 0.8 %copy-done.5 = bf16[16,2048]{1,0:T(8,128)(2,1)S(1)} copy-done((bf16[16,2048]{1,0:T(8,128)(2,1)S(1)}, bf16[16,2048]{1,0:T(8,128)(2,1)}, u32[]{:S(2)}) %copy-start.5) | copy-done | bytes 65560
  8.6 0.0 copy-start.6
  8.6 0.8 %copy-done.6 = bf16[16,2048]{1,0:T(8,128)(2,1)S(1)} copy-done((bf16[16,2048]{1,0:T(8,128)(2,1)S(1)}, bf16[16,2048]{1,0:T(8,128)(2,1)}, u32[]{:S(2)}) %copy-start.6) | copy-done | bytes 65560
  9.4 51.2 %shard_map.120 = (bf16[384,128]{1,0:T(8,128)(2,1)S(1)}, bf16[384,128]{1,0:T(8,128)(2,1)S(1)}, bf16[384,1024]{1,0:T(8,128)(2,1)S(1)}, bf16[32,512]{1,0:T(8,128)(2,1)S(1)}) custom-call(bf16[16,2048]{1,0:T(8,128)(2,1)S(1)} %copy-done.5, bf16[16,2048]{1,0:T(8,128)(2,1)S(1)} %copy-done.6, bf16[384,128]{1,0:T(8,128)(2,1)S(1)} %copy-done.3, ...), custom_call_target="tpu_custom_call" | custom-call | tf_op jit(solution)/shard_map/pallas_call | solution.py:380
  60.6 0.6 %copy.19 = bf16[384,128]{1,0:T(8,128)(2,1)} copy(bf16[384,128]{1,0:T(8,128)(2,1)S(1)} %get-tuple-element.8) | data formatting | bytes 196608
  61.3 0.6 %copy.20 = bf16[384,128]{1,0:T(8,128)(2,1)} copy(bf16[384,128]{1,0:T(8,128)(2,1)S(1)} %get-tuple-element.9) | data formatting | bytes 196608
  61.9 0.9 %copy.21 = bf16[384,1024]{1,0:T(8,128)(2,1)} copy(bf16[384,1024]{1,0:T(8,128)(2,1)S(1)} %get-tuple-element.10) | data formatting | bytes 1572864
  62.8 0.6 copy.22
Async XLA Ops:
  1.9 1.6 %copy-start = (bf16[512,2048]{1,0:T(8,128)(2,1)S(1)}, bf16[512,2048]{1,0:T(8,128)(2,1)}, u32[]{:S(2)}) copy-start(bf16[512,2048]{1,0:T(8,128)(2,1)} %wq_in.1) | copy-start | bytes 6291460
  3.5 1.2 %copy-start.1 = (bf16[4096,128]{1,0:T(8,128)(2,1)S(1)}, bf16[4096,128]{1,0:T(8,128)(2,1)}, u32[]{:S(2)}) copy-start(bf16[4096,128]{1,0:T(8,128)(2,1)} %kw_in.1) | copy-start | bytes 3145732
  4.7 1.2 %copy-start.2 = (bf16[4096,128]{1,0:T(8,128)(2,1)S(1)}, bf16[4096,128]{1,0:T(8,128)(2,1)}, u32[]{:S(2)}) copy-start(bf16[4096,128]{1,0:T(8,128)(2,1)} %vw_in.1) | copy-start | bytes 3145732
  6.0 0.9 %copy-start.3 = (bf16[384,128]{1,0:T(8,128)(2,1)S(1)}, bf16[384,128]{1,0:T(8,128)(2,1)}, u32[]{:S(2)}) copy-start(bf16[384,128]{1,0:T(8,128)(2,1)} %k_ref.1) | copy-start | bytes 294916
  6.9 0.9 %copy-start.4 = (bf16[384,128]{1,0:T(8,128)(2,1)S(1)}, bf16[384,128]{1,0:T(8,128)(2,1)}, u32[]{:S(2)}) copy-start(bf16[384,128]{1,0:T(8,128)(2,1)} %v_ref.1) | copy-start | bytes 294916
  7.8 0.8 %copy-start.5 = (bf16[16,2048]{1,0:T(8,128)(2,1)S(1)}, bf16[16,2048]{1,0:T(8,128)(2,1)}, u32[]{:S(2)}) copy-start(bf16[16,2048]{1,0:T(8,128)(2,1)} %q_in.1) | copy-start | bytes 196612
  8.6 0.8 %copy-start.6 = (bf16[16,2048]{1,0:T(8,128)(2,1)S(1)}, bf16[16,2048]{1,0:T(8,128)(2,1)}, u32[]{:S(2)}) copy-start(bf16[16,2048]{1,0:T(8,128)(2,1)} %g_in.1) | copy-start | bytes 196612

commit v2 on v1

--- a/solution.py
+++ b/solution.py
@@ -27,9 +27,9 @@
 
 def kernel(
     n, nh,
-    q_in, g_in, k_ref, v_ref, len_ref, span_ref, wq_in, kw_in, vw_in,
+    q_in, g_in, k_in, v_in, len_ref, span_ref, wq_in, kw_in, vw_in,
     dk_out, dv_out, cached_out, span_out,
-    q_all, g_all, kt, len_all, bias, e_buf, dp_buf, st_all, fac, rterm,
+    q_all, g_all, k_ref, v_ref, kt, len_all, bias, e_buf, dp_buf, st_all, fac, rterm,
     dv_acc, dk_acc, dq_send, dq_recv, dq_all, wq, w_all, dkv_all, acc,
     span_acc, span_send, span_recv,
     loc_sem, q_sem, g_sem, a_sem, len_sem, st_sem, rs_sem, w_sem, wf_sem, z_sem, h_sem,
@@ -40,7 +40,7 @@
     sib = me + 1 - 2 * core
     rows_own = q_in.shape[0]
     rows = rows_own * n
-    slots = k_ref.shape[0]
+    slots = k_in.shape[0]
     heads = q_in.shape[1] // HEAD_WIDTH
     hb = heads // n
     wid = hb * HEAD_WIDTH
@@ -75,6 +75,8 @@
         pltpu.make_async_copy(wq_in, wq, loc_sem.at[2]),
         pltpu.make_async_copy(kw_in.at[own_feats], w_all.at[2 * hd], loc_sem.at[3]),
         pltpu.make_async_copy(vw_in.at[own_feats], w_all.at[2 * hd + 1], loc_sem.at[4]),
+        pltpu.make_async_copy(k_in, k_ref, loc_sem.at[5]),
+        pltpu.make_async_copy(v_in, v_ref, loc_sem.at[6]),
     ]
     for c in local:
         c.start()
@@ -156,7 +158,9 @@
         for which in range(2):
             weight_copy(k, which).start()
 
+    local[5].wait()
     kt[...] = k_ref[...].T
+    local[6].wait()
     gather_relay(*q_args)
     gather_relay(*g_args)
 
@@ -257,12 +261,33 @@
     dkv_all[2 * hd] = dk_low
     dkv_all[2 * hd + 1] = dv_low
 
-    def z_copy(k):
-        block = dkv_all.at[pl.ds(2 * hd, 2)]
-        return remote(block, block, z_sem.at[0, k], z_sem.at[1, k], me, head_peer(k))
-
-    for k in range(1, nh):
-        z_copy(k).start()
+    def z_send(way, d):
+        src = hd - (d - 1) if way == 0 else hd + (d - 1)
+        to = hd + 1 if way == 0 else hd - 1
+        block = dkv_all.at[pl.ds(2 * src, 2)]
+        ok = (src >= 0) & (src < nh) & (to >= 0) & (to < nh)
+        return ok, remote(block, block, z_sem.at[0, way, d], z_sem.at[1, way, d], me, to)
+
+    def z_recv(way, d):
+        src = hd - d if way == 0 else hd + d
+        block = dkv_all.at[pl.ds(2 * src, 2)]
+        ok = (src >= 0) & (src < nh)
+        return ok, src, remote(
+            block, block, z_sem.at[0, way, d], z_sem.at[1, way, d], me, head_peer(1)
+        )
+
+    def z_start(d):
+        for way in range(2):
+            ok, c = z_send(way, d)
+            pl.when(ok)(c.start)
+
+    def z_hop(d):
+        for way in range(2):
+            ok, _, c = z_recv(way, d - 1)
+            pl.when(ok)(c.wait_recv)
+        z_start(d)
+
+    z_start(1)
     dk_out[...] = dk_low
     dv_out[...] = dv_low
 
@@ -276,6 +301,7 @@
         )
     gather_start(*a_args)
 
+    z_hop(2)
     for k in range(1, nh):
         weight_copy(k, 0).wait_recv()
         weight_copy(k, 1).wait_recv()
@@ -285,26 +311,21 @@
     local[4].wait()
     tile = min(256, feats)
 
-    def term(g, start, last):
+    def term(g, start):
         lhs = jnp.concatenate([dkv_all[2 * g], dkv_all[2 * g + 1]], axis=1)
 
         def one(i, carry):
             at = pl.ds(pl.multiple_of(i * tile, tile), tile)
             rhs = jnp.concatenate([w_all[2 * g, at, :], w_all[2 * g + 1, at, :]], axis=1)
             x = dot_nt(lhs, rhs)
-            if not start:
-                x = x + acc[:, at]
-            if last:
-                cached_out[:, at] = x.astype(cached_out.dtype)
-            else:
-                acc[:, at] = x
+            acc[:, at] = x if start else x + acc[:, at]
             return carry
 
         lax.fori_loop(0, feats // tile, one, 0)
 
     local[2].wait()
     gather_relay(*a_args)
-    term(hd, True, nh == 1)
+    term(hd, True)
 
     def span_add(s):
         cols = pl.ds(pl.multiple_of(s * wid, wid), wid)
@@ -331,10 +352,21 @@
     for k in range(1, nh):
         h_copy(k).start()
 
+    for d in range(3, nh):
+        z_hop(d)
     for k in range(1, nh):
         weight_forward(k).wait_recv()
-        z_copy(k).wait_recv()
-        term(head_from(k), False, k == nh - 1)
+    for d in range(1, nh):
+        for way in range(2):
+            ok, src, c = z_recv(way, d)
+
+            @pl.when(ok)
+            def _(src=src, c=c, d=d, way=way):
+                if d == nh - 1:
+                    c.wait_recv()
+                term(src, False)
+
+    cached_out[...] = acc[...].astype(cached_out.dtype)
 
     own_span = pl.ds(pl.multiple_of(hd * span_rows, span_rows), span_rows)
     total = span_acc[own_span, :]
@@ -355,7 +387,9 @@
         weight_copy(k, 0).wait_send()
         weight_copy(k, 1).wait_send()
         weight_forward(k).wait_send()
-        z_copy(k).wait_send()
+        for way in range(2):
+            ok, c = z_send(way, k)
+            pl.when(ok)(c.wait_send)
         h_copy(k).wait_send()
 
 
@@ -373,11 +407,11 @@
     bf, f32 = jnp.bfloat16, jnp.float32
     vmem = pl.BlockSpec(memory_space=pltpu.VMEM)
     smem = pl.BlockSpec(memory_space=pltpu.SMEM)
-    anym = pl.BlockSpec(memory_space=pl.ANY)
+    hbm = pl.BlockSpec(memory_space=pltpu.HBM)
     dma = pltpu.SemaphoreType.DMA
     V = pltpu.VMEM
     hq = wid // HEAD_WIDTH * rows
-    return pl.pallas_call(
+    results = pl.pallas_call(
         functools.partial(kernel, n, nh),
         out_shape=(
             jax.ShapeDtypeStruct((slots, HEAD_WIDTH), bf),
@@ -385,11 +419,13 @@
             jax.ShapeDtypeStruct((slots, feats), bf),
             jax.ShapeDtypeStruct((rows // nh, out_feats), bf),
         ),
-        in_specs=[anym, anym, vmem, vmem, smem, smem, anym, anym, anym],
+        in_specs=[hbm, hbm, hbm, hbm, smem, smem, hbm, hbm, hbm],
         out_specs=(vmem, vmem, vmem, vmem),
         scratch_shapes=[
             V((rows, width), bf),
             V((rows, width), bf),
+            V((slots, HEAD_WIDTH), bf),
+            V((slots, HEAD_WIDTH), bf),
             V((HEAD_WIDTH, slots), bf),
             V((n, 8, 128), jnp.int32),
             V((slots, rows), f32),
@@ -410,7 +446,7 @@
             V((rows, out_feats), f32),
             V((nh, rows // nh, out_feats), bf),
             V((nh, rows // nh, out_feats), bf),
-            dma((5,)),
+            dma((7,)),
             dma((4, nchip)),
             dma((4, nchip)),
             dma((4, nchip)),
@@ -419,16 +455,35 @@
             dma((2, n)),
             dma((2, 2, nh)),
             dma((2, nh)),
-            dma((2, nh)),
+            dma((2, 2, nh)),
             dma((2, nh)),
         ],
         compiler_params=pltpu.CompilerParams(
-            collective_id=0, has_side_effects=True, vmem_limit_bytes=48 * 1024 * 1024
+            collective_id=0, has_side_effects=True, vmem_limit_bytes=63 * 1024 * 1024
         ),
     )(
         queries, grad_output, key_cache, saved_value_rows, lengths, span_index,
         w_query, key_projection_weight, value_projection_weight,
     )
+    count = len(results)
+    return pl.pallas_call(
+        functools.partial(write_out, count),
+        out_shape=tuple(jax.ShapeDtypeStruct(r.shape, r.dtype) for r in results),
+        in_specs=[vmem] * count,
+        out_specs=(hbm,) * count,
+        scratch_shapes=[dma((count,))],
+    )(*results)
+
+
+def write_out(count, *refs):
+    sem = refs[-1]
+    copies = [
+        pltpu.make_async_copy(refs[i], refs[count + i], sem.at[i]) for i in range(count)
+    ]
+    for c in copies:
+        c.start()
+    for c in copies:
+        c.wait()
 
 
 def prefix(part, axis, combine, identity):
@@ -584,6 +639,8 @@
             and heads % n == 0
             and (heads // 2) % 8 == 0
             and (rows // nh) % 16 == 0
+            and nh >= 3
+            and rest[-1].shape[0] % (nh * n * 16) == 0
         )
         if not fits:
             return local(queries, *rest)

time: 63.8 us -> 54.1 us (0.85)
  local copies, waits for them, and re-layouts: 10.3 us -> 0 us
  Pallas kernels: 51.2 us -> 52 us
    unnamed x18 -> x0, local copies, waits for them, and re-layouts: 10.3 us -> none
    pallas_call x0 -> x1, Pallas kernels: none -> 2.23 us  [fused(): pl.pallas_call(functools.partial(write_out, count), out_shape=tuple((jax....]
    pallas_call x1, Pallas kernels: 51.2 us -> 49.8 us  [fused(): pl.pallas_call(functools.partial(kernel, n, nh), out_shape=(jax.ShapeDtyp...]
where the time goes in v2:
time: 54.1 us; the launch traced here: 53.9 us
  Pallas kernels  52 us (96%)
  between operations  1.93 us (4%)
    pallas_call x1, Pallas kernels, fused(): pl.pallas_call(functools.partial(kernel, n, nh), out_shape=(jax.ShapeDtyp...  49.8 us
    pallas_call x1, Pallas kernels, fused(): pl.pallas_call(functools.partial(write_out, count), out_shape=tuple((jax....  2.23 us

profile of v2, /device:TPU:0, one launch (start us, length us, event | category | flops | bytes accessed | tf_op | source)
XLA Modules:
  0.0 53.9 jit_solution(12130483583222403017)
XLA Ops:
  1.9 49.8 %shard_map.120 = (bf16[384,128]{1,0:T(8,128)(2,1)}, bf16[384,128]{1,0:T(8,128)(2,1)}, bf16[384,1024]{1,0:T(8,128)(2,1)}, bf16[32,512]{1,0:T(8,128)(2,1)}) custom-call(bf16[16,2048]{1,0:T(8,128)(2,1)} %q_in.1, bf16[16,2048]{1,0:T(8,128)(2,1)} %g_in.1, bf16[384,128]{1,0:T(8,128)(2,1)} %k_in.1, bf16[384,128]{1,0:T(8,128)(2,1)} %v_in.1, s32[1]{0:T(128)S(6)} %copy.13.len_ref, ...), custom_call_target="tpu_custom_call" | custom-call | tf_op jit(solution)/shard_map/pallas_call | solution.py:414
  51.7 2.2 %shard_map.121 = (bf16[384,128]{1,0:T(8,128)(2,1)}, bf16[384,128]{1,0:T(8,128)(2,1)}, bf16[384,1024]{1,0:T(8,128)(2,1)}, bf16[32,512]{1,0:T(8,128)(2,1)}) custom-call(bf16[384,128]{1,0:T(8,128)(2,1)} %get-tuple-element.8.refs_0_, bf16[384,128]{1,0:T(8,128)(2,1)} %get-tuple-element.9.refs_1_, bf16[384,1024]{1,0:T(8,128)(2,1)} %get-tuple-element.10.refs_2_, ...), custom_call_target="tpu_custom_call" | custom-call | tf_op jit(solution)/shard_map/pallas_call | solution.py:469

commit v3 on v2

--- a/solution.py
+++ b/solution.py
@@ -78,8 +78,8 @@
         pltpu.make_async_copy(k_in, k_ref, loc_sem.at[5]),
         pltpu.make_async_copy(v_in, v_ref, loc_sem.at[6]),
     ]
-    for c in local:
-        c.start()
+    for i in (0, 1, 5, 6):
+        local[i].start()
     len_all[me] = jnp.full((8, 128), len_ref[0], jnp.int32)
 
     barrier = pltpu.get_barrier_semaphore()
@@ -135,10 +135,6 @@
             len_all.at[me], len_all.at[me], len_sem.at[0, k], len_sem.at[1, k], seq_peer(k), hd
         )
 
-    gather_start(*q_args)
-    for k in range(1, n):
-        len_copy(k).start()
-    gather_start(*g_args)
 
     core_feats = pl.ds(pl.multiple_of(core * fh, fh), fh)
 
@@ -157,6 +153,13 @@
     for k in range(1, nh):
         for which in range(2):
             weight_copy(k, which).start()
+    gather_start(*q_args)
+    for k in range(1, n):
+        len_copy(k).start()
+    gather_start(*g_args)
+
+    for i in (3, 4, 2):
+        local[i].start()
 
     local[5].wait()
     kt[...] = k_ref[...].T
@@ -261,33 +264,35 @@
     dkv_all[2 * hd] = dk_low
     dkv_all[2 * hd + 1] = dv_low
 
-    def z_send(way, d):
+    def z_send(way, d, w):
         src = hd - (d - 1) if way == 0 else hd + (d - 1)
         to = hd + 1 if way == 0 else hd - 1
-        block = dkv_all.at[pl.ds(2 * src, 2)]
+        block = dkv_all.at[2 * src + w]
         ok = (src >= 0) & (src < nh) & (to >= 0) & (to < nh)
-        return ok, remote(block, block, z_sem.at[0, way, d], z_sem.at[1, way, d], me, to)
-
-    def z_recv(way, d):
+        return ok, remote(block, block, z_sem.at[0, way, d, w], z_sem.at[1, way, d, w], me, to)
+
+    def z_recv(way, d, w):
         src = hd - d if way == 0 else hd + d
-        block = dkv_all.at[pl.ds(2 * src, 2)]
+        block = dkv_all.at[2 * src + w]
         ok = (src >= 0) & (src < nh)
         return ok, src, remote(
-            block, block, z_sem.at[0, way, d], z_sem.at[1, way, d], me, head_peer(1)
-        )
-
-    def z_start(d):
+            block, block, z_sem.at[0, way, d, w], z_sem.at[1, way, d, w], me, head_peer(1)
+        )
+
+    def z_start(d, w):
         for way in range(2):
-            ok, c = z_send(way, d)
+            ok, c = z_send(way, d, w)
             pl.when(ok)(c.start)
 
-    def z_hop(d):
+    def z_hop(d, w):
         for way in range(2):
-            ok, _, c = z_recv(way, d - 1)
+            ok, _, c = z_recv(way, d - 1, w)
             pl.when(ok)(c.wait_recv)
-        z_start(d)
-
-    z_start(1)
+            ok, c = z_send(way, d, w)
+            pl.when(ok)(c.start)
+
+    z_start(1, 1)
+    z_start(1, 0)
     dk_out[...] = dk_low
     dv_out[...] = dv_low
 
@@ -301,7 +306,8 @@
         )
     gather_start(*a_args)
 
-    z_hop(2)
+    z_hop(2, 1)
+    z_hop(2, 0)
     for k in range(1, nh):
         weight_copy(k, 0).wait_recv()
         weight_copy(k, 1).wait_recv()
@@ -353,17 +359,20 @@
         h_copy(k).start()
 
     for d in range(3, nh):
-        z_hop(d)
+        z_hop(d, 1)
+        z_hop(d, 0)
     for k in range(1, nh):
         weight_forward(k).wait_recv()
     for d in range(1, nh):
         for way in range(2):
-            ok, src, c = z_recv(way, d)
+            ok, src, last_v = z_recv(way, d, 1)
+            last_k = z_recv(way, d, 0)[2]
 
             @pl.when(ok)
-            def _(src=src, c=c, d=d, way=way):
+            def _(src=src, last_v=last_v, last_k=last_k, d=d):
                 if d == nh - 1:
-                    c.wait_recv()
+                    last_v.wait_recv()
+                    last_k.wait_recv()
                 term(src, False)
 
     cached_out[...] = acc[...].astype(cached_out.dtype)
@@ -388,8 +397,9 @@
         weight_copy(k, 1).wait_send()
         weight_forward(k).wait_send()
         for way in range(2):
-            ok, c = z_send(way, k)
-            pl.when(ok)(c.wait_send)
+            for w in range(2):
+                ok, c = z_send(way, k, w)
+                pl.when(ok)(c.wait_send)
         h_copy(k).wait_send()
 
 
@@ -455,7 +465,7 @@
             dma((2, n)),
             dma((2, 2, nh)),
             dma((2, nh)),
-            dma((2, 2, nh)),
+            dma((2, 2, nh, 2)),
             dma((2, nh)),
         ],
         compiler_params=pltpu.CompilerParams(

time: 54.1 us -> 53.7 us (level)
  no operation moved by 1% of the time
where the time goes in v3:
time: 53.7 us; the launch traced here: 53.5 us
  Pallas kernels  51.6 us (96%)
  between operations  1.93 us (4%)
    pallas_call x1, Pallas kernels, fused(): pl.pallas_call(functools.partial(kernel, n, nh), out_shape=(jax.ShapeDtyp...  49.4 us
    pallas_call x1, Pallas kernels, fused(): pl.pallas_call(functools.partial(write_out, count), out_shape=tuple((jax....  2.23 us

profile of v3, /device:TPU:0, one launch (start us, length us, event | category | flops | bytes accessed | tf_op | source)
XLA Modules:
  0.0 53.5 jit_solution(5742115331374570631)
XLA Ops:
  1.9 49.4 %shard_map.120 = (bf16[384,128]{1,0:T(8,128)(2,1)}, bf16[384,128]{1,0:T(8,128)(2,1)}, bf16[384,1024]{1,0:T(8,128)(2,1)}, bf16[32,512]{1,0:T(8,128)(2,1)}) custom-call(bf16[16,2048]{1,0:T(8,128)(2,1)} %q_in.1, bf16[16,2048]{1,0:T(8,128)(2,1)} %g_in.1, bf16[384,128]{1,0:T(8,128)(2,1)} %k_in.1, bf16[384,128]{1,0:T(8,128)(2,1)} %v_in.1, s32[1]{0:T(128)S(6)} %copy.13.len_ref, ...), custom_call_target="tpu_custom_call" | custom-call | tf_op jit(solution)/shard_map/pallas_call | solution.py:424
  51.3 2.2 %shard_map.121 = (bf16[384,128]{1,0:T(8,128)(2,1)}, bf16[384,128]{1,0:T(8,128)(2,1)}, bf16[384,1024]{1,0:T(8,128)(2,1)}, bf16[32,512]{1,0:T(8,128)(2,1)}) custom-call(bf16[384,128]{1,0:T(8,128)(2,1)} %get-tuple-element.8.refs_0_, bf16[384,128]{1,0:T(8,128)(2,1)} %get-tuple-element.9.refs_1_, bf16[384,1024]{1,0:T(8,128)(2,1)} %get-tuple-element.10.refs_2_, ...), custom_call_target="tpu_custom_call" | custom-call | tf_op jit(solution)/shard_map/pallas_call | solution.py:479
